TPU v7x, 32 devices: a whole 2x2x4 slice. The times are simulated.
32 devices in a mesh: seq: 8 (over z, y), head: 4 (over x, core).
Axes of the slice: x: 2, y: 2, z: 4, core: 2. Of those that a mesh axis runs over, the one named last changes fastest.
Arguments:
- tokens: bfloat16 [16384, 1024], P(('seq', 'head')), may hold values from -6 to 6
- w_gate_x: bfloat16 [1024, 4096], replicated, may hold values from -0.1875 to 0.1875
- w_bc_dt: bfloat16 [1024, 160], replicated, may hold values from -0.1875 to 0.1875
- conv_x_weight: float32 [4, 2048], P(None, 'head'), may hold values from -0.5 to 0.5
- conv_x_bias: float32 [2048], P('head'), may hold values from -0.5 to 0.5
- conv_bc_weight: float32 [4, 128], replicated, may hold values from -0.5 to 0.5
- conv_bc_bias: float32 [128], replicated, may hold values from -0.5 to 0.5
- dt_bias: float32 [32], P('head'), may hold values from -9 to -1
- a_log: float32 [32], P('head'), may hold values from -4 to 1
- skip_d: float32 [32], P('head'), may hold values from 0.5 to 1.5
- norm_gain: float32 [2048], replicated, may hold values from 0.1 to 1.9
- w_out: bfloat16 [2048, 1024], replicated, may hold values from -0.125 to 0.125
Outputs:
- mixed: bfloat16 [16384, 1024], P(('seq', 'head'))
All inputs are finite; a program needn't handle non-finite values.
Results may differ from a plain program's by a relative error of at most 0.009.
Values may be sent and summed in bfloat16 or wider, within the bound.
A program may use at most 128 MiB of HBM per device.

v0:
```python
import jax
import jax.numpy as jnp
from jax import lax
from jax.sharding import PartitionSpec as P

HEADS = 32
HEAD_DIM = 64
STATE = 64
GROUP = 256
CONV = 4


epsilon = 1e-05


def from_behind(array, axis, by):
    size = lax.axis_size(axis)
    pairs = [(i, i + by) for i in range(size) if 0 <= i + by < size]
    return lax.ppermute(array, axis, pairs)


def prefix(array, axis, combine, identity):
    size, mine = (lax.axis_size(axis), lax.axis_index(axis))
    everything = jax.tree.map(lambda part: lax.all_gather(part, axis), array)
    start = jax.tree.map(
        lambda part, zero: jnp.broadcast_to(jnp.asarray(zero, part.dtype), part.shape),
        array,
        identity,
    )

    def hop(k, before):
        reached = k < mine
        new = combine(before, jax.tree.map(lambda part: part[k], everything))
        return jax.tree.map(lambda a, b: jnp.where(reached, a, b), new, before)

    return lax.fori_loop(0, size, hop, start)


def causal_taps(padded, weights, biases, count):
    summed = biases + weights[0] * padded[0:count]
    for tap_index in range(1, CONV):
        summed = summed + weights[tap_index] * padded[tap_index : tap_index + count]
    return jax.nn.silu(summed).astype(jnp.bfloat16)


def on_device(
    tokens,
    w_gate_x,
    w_bc_dt,
    conv_x_weight,
    conv_x_bias,
    conv_bc_weight,
    conv_bc_bias,
    dt_bias,
    a_log,
    skip_d,
    norm_gain,
    w_out,
):
    highest = lax.Precision.HIGHEST
    heads_here = dt_bias.shape[0]
    dinner_here = heads_here * HEAD_DIM
    tok_rows = tokens.shape[0]
    gate_all = jnp.dot(tokens, w_gate_x, preferred_element_type=jnp.float32).astype(jnp.bfloat16)
    gate_all = gate_all.reshape(tok_rows, HEADS, 2 * HEAD_DIM)
    bc_dt = jnp.dot(tokens, w_bc_dt, preferred_element_type=jnp.float32).astype(jnp.bfloat16)
    dt_all = bc_dt[:, 2 * STATE :].reshape(tok_rows, HEADS, 1)
    gate_x, dt_raw = (
        lax.all_to_all(gate_all, "head", split_axis=1, concat_axis=0, tiled=True),
        lax.all_to_all(dt_all, "head", split_axis=1, concat_axis=0, tiled=True),
    )
    dt_raw = dt_raw[:, :, 0]
    bc_rows = lax.all_gather(bc_dt[:, : 2 * STATE], "head", axis=0, tiled=True)
    seq_rows = gate_x.shape[0]
    gate_z = gate_x[:, :, :HEAD_DIM]
    x_chan = gate_x[:, :, HEAD_DIM:].reshape(seq_rows, dinner_here)
    conv_input = jnp.concatenate([x_chan, bc_rows], axis=1)
    rim_rows = from_behind(conv_input[seq_rows - (CONV - 1) :], "seq", 1)
    padded = jnp.concatenate([rim_rows, conv_input], axis=0).astype(jnp.float32)
    conv_weights = jnp.concatenate([conv_x_weight, conv_bc_weight], axis=1)
    conv_biases = jnp.concatenate([conv_x_bias, conv_bc_bias], axis=0)
    conved = causal_taps(padded, conv_weights, conv_biases, seq_rows)
    x_heads = conved[:, :dinner_here].astype(jnp.float32).reshape(seq_rows, heads_here, HEAD_DIM)
    b_mat = conved[:, dinner_here : dinner_here + STATE].astype(jnp.float32)
    c_mat = conved[:, dinner_here + STATE :].astype(jnp.float32)
    dt_step = jax.nn.softplus(dt_raw.astype(jnp.float32) + dt_bias)
    log_decay = dt_step * -jnp.exp(a_log)
    x_dt = x_heads * dt_step[:, :, None]
    blocks = seq_rows // GROUP
    decay_blocks = log_decay.reshape(blocks, GROUP, heads_here)
    xdt_blocks = x_dt.reshape(blocks, GROUP, heads_here, HEAD_DIM)
    b_blocks = b_mat.reshape(blocks, GROUP, STATE)
    c_blocks = c_mat.reshape(blocks, GROUP, STATE)
    cumlog = jnp.cumsum(decay_blocks, axis=1)
    scores = jnp.einsum("ktn,ksn->kts", c_blocks, b_blocks, precision=highest)
    by_head = jnp.swapaxes(cumlog, 1, 2)
    gaps = by_head[:, :, :, None] - by_head[:, :, None, :]
    causal = jnp.arange(GROUP)[:, None] >= jnp.arange(GROUP)[None, :]
    decays = jnp.where(causal[None, None], jnp.exp(jnp.minimum(gaps, 0.0)), 0.0)
    mixed = scores[:, None] * decays
    y_intra = jnp.einsum("khts,kshp->kthp", mixed, xdt_blocks, precision=highest)
    block_ends = cumlog[:, -1, :]
    to_end = jnp.exp(block_ends[:, None, :] - cumlog)
    local_states = jnp.einsum(
        "kshp,ksn->khpn", to_end[..., None] * xdt_blocks, b_blocks, precision=highest
    )

    def chain_step(carried, inputs):
        block_decay, fresh = inputs
        return (block_decay[:, None, None] * carried + fresh, carried)

    zero_state = jnp.zeros((heads_here, HEAD_DIM, STATE), jnp.float32)
    device_state, block_starts = lax.scan(
        chain_step, zero_state, (jnp.exp(block_ends), local_states)
    )
    total_log = jnp.sum(block_ends, axis=0)

    def combine(earlier, latter):
        return (earlier[0] + latter[0], earlier[1] * jnp.exp(latter[0])[:, None, None] + latter[1])

    prefix_log, incoming = prefix(
        (total_log, device_state), "seq", combine, (jnp.zeros_like(total_log), zero_state)
    )
    offset = jnp.cumsum(block_ends, axis=0) - block_ends
    start_states = block_starts + jnp.exp(offset)[:, :, None, None] * incoming[None]
    y_state = jnp.exp(cumlog)[..., None] * jnp.einsum(
        "ktn,khpn->kthp", c_blocks, start_states, precision=highest
    )
    y_heads = (y_intra + y_state).reshape(seq_rows, heads_here, HEAD_DIM) + skip_d[
        None, :, None
    ] * x_heads
    gated_out = (
        (y_heads * jax.nn.silu(gate_z.astype(jnp.float32)))
        .astype(jnp.bfloat16)
        .reshape(seq_rows, dinner_here)
    )
    by_token = lax.all_to_all(gated_out, "head", split_axis=0, concat_axis=1, tiled=True)
    gated_f = by_token.astype(jnp.float32)
    mean_sq = jnp.mean(gated_f * gated_f, axis=1, keepdims=True)
    normed = (gated_f * lax.rsqrt(mean_sq + epsilon) * norm_gain).astype(jnp.bfloat16)
    return jnp.dot(normed, w_out, preferred_element_type=jnp.float32).astype(jnp.bfloat16)


def solution(mesh):
    return jax.shard_map(
        on_device,
        mesh=mesh,
        in_specs=(
            P(("seq", "head"), None),
            P(),
            P(),
            P(None, "head"),
            P("head"),
            P(),
            P(),
            P("head"),
            P("head"),
            P("head"),
            P(),
            P(),
        ),
        out_specs=P(("seq", "head"), None),
        check_vma=False,
    )
```

profile of v0, /device:TPU:0, one launch (start us, length us, event | category | flops | bytes accessed | tf_op | source)
XLA Modules:
  0.0 248.3 jit_solution(16205255267855626271)
XLA Ops:
  6.5 1.2 copy-done
  7.8 1.5 convolution_convert_fusion.2
  9.8 0.8 reduce.13
  11.3 4.2 %all-to-all-start.1 = ((bf16[4,2,2048]{2,1,0:T(2,128)(2,1)}), bf16[4,2,2048]{2,1,0:T(2,128)(2,1)S(1)}, u32[]{:S(2)}, u32[]{:S(2)}) async-start(bf16[4,2,2048]{2,1,0:T(2,128)(2,1)} %reshape.184), calls=%async_computation.1 | async-start | bytes 65536 | tf_op jit(solution)/shard_map/all_to_all | solution.py:70
  15.5 8.1 %fusion.28 = bf16[64,32,8,128]{3,2,1,0:T(8,128)(2,1)S(1)} fusion(bf16[512,1024]{1,0:T(8,128)(2,1)S(1)} %copy-done, bf16[1024,4096]{1,0:T(8,128)(2,1)} %param.17), kind=kOutput, calls=%fused_computation.46 | convolution fusion | flops 4297064448 | bytes 13631488 | tf_op jit(solution)/shard_map/dot_general | solution.py:64
  23.6 3.1 %copy.123 = bf16[64,32,8,128]{3,2,0,1:T(8,128)(2,1)} copy(bf16[64,32,8,128]{3,2,1,0:T(8,128)(2,1)S(1)} %fusion.28) | data formatting | bytes 8388608 | tf_op jit(solution)/shard_map/reshape | solution.py:65
  26.8 5.0 %all-to-all-start = ((bf16[512,32,128]{2,0,1:T(8,128)(2,1)}), bf16[512,32,128]{2,0,1:T(8,128)(2,1)}, u32[]{:S(2)}, u32[]{:S(2)}) async-start(bf16[512,32,128]{2,0,1:T(8,128)(2,1)} %bitcast.113), calls=%async_computation | async-start | bytes 8388608 | tf_op jit(solution)/shard_map/all_to_all | solution.py:69
  32.0 51.6 %all_gather.15 = bf16[2048,128]{0,1:T(8,128)(2,1)S(1)} all-gather(bf16[512,128]{0,1:T(8,128)(2,1)S(1)} %slice.78), channel_id=1, replica_groups=mesh['seq'=8,'head'=4] {'head'}, dimensions={0}, use_global_device_ids=true | all-gather | bytes 655360 | tf_op jit(solution)/shard_map/all_gather | solution.py:73
  83.8 4.5 %reduce-window.6 = f32[8,8,2,128]{3,1,2,0:T(8,128)S(1)} reduce-window(f32[8,8,2,128]{3,1,2,0:T(8,128)S(1)} %get-tuple-element.196, f32[]{:T(128)} %constant.58.clone.1), window={size=1x1x1x128 pad=0_0x0_0x0_0x127_0}, to_apply=%region_0.1 | reduce-window | flops 2080768 | bytes 131076 | tf_op jit(solution)/shard_map/reduce-window
  89.1 4.9 %copy.73 = bf16[4,512,8,128]{3,2,1,0:T(8,128)(2,1)S(1)} copy(bf16[4,512,8,128]{3,1,2,0:T(8,128)(2,1)} %bitcast.2) | data formatting | bytes 8388608 | tf_op jit(solution)/shard_map/all_to_all | solution.py:69
  94.0 4.0 %fusion.44 = (bf16[2048,8,64]{2,1,0:T(8,128)(2,1)}, bf16[2048,8,64]{2,1,0:T(8,128)(2,1)}) fusion(bf16[2048,8,128]{2,1,0:T(8,128)(2,1)S(1)} %bitcast.109), kind=kLoop, calls=%fused_computation.87 | loop fusion | bytes 8388608 | tf_op jit(solution)/shard_map/slice | solution.py:76
  98.0 4.5 %copy.74 = bf16[2048,8,64]{0,2,1:T(8,128)(2,1)S(1)} copy(bf16[2048,8,64]{2,1,0:T(8,128)(2,1)} %get-tuple-element.198) | data formatting | bytes 4194304 | tf_op jit(solution)/shard_map/slice | solution.py:76
  102.6 4.1 %collective-permute-start = (bf16[3,640]{0,1:T(8,128)(2,1)S(1)}, bf16[3,640]{0,1:T(8,128)(2,1)S(1)}, u32[]{:S(2)}, u32[]{:S(2)}) collective-permute-start(bf16[3,640]{0,1:T(8,128)(2,1)S(1)} %pad_maximum_fusion), channel_id=1, source_target_pairs={{0,4},{4,8},{8,12},{12,16},{16,20},{20,24},{24,28},{1,5},{5,9},{9,... | collective-permute-start | bytes 11528 | tf_op jit(solution)/shard_map/ppermute | solution.py:19
  106.8 3.7 %collective-permute-done = bf16[3,640]{0,1:T(8,128)(2,1)S(1)} collective-permute-done((bf16[3,640]{0,1:T(8,128)(2,1)S(1)}, bf16[3,640]{0,1:T(8,128)(2,1)S(1)}, u32[]{:S(2)}, u32[]{:S(2)}) %collective-permute-start) | collective-permute-done | bytes 3872 | tf_op jit(solution)/shard_map/ppermute | solution.py:19
  110.5 1.1 maximum_convert_fusion
  111.6 5.2 %multiply_convert_fusion = bf16[2048,640]{0,1:T(8,128)(2,1)S(1)} fusion(f32[2051,640]{0,1:T(8,128)S(1)} %maximum_convert_fusion, f32[640]{0:T(1024)S(1)} %get-tuple-element.169, f32[640]{0:T(1024)S(1)} %get-tuple-element.170, f32[640]{0:T(1024)S(1)} %get-tuple-element.171, f32[640]{0:T(1024)S(1)} %get-tuple-element.168, f32[640]{0:T(1024)S(1)} %pad_maximum_fusion.1), kind=kLoop, calls=%fused_computation.29 | loop fusion | flops 17039360 | bytes 23605760 | tf_op jit(solution)/shard_map/convert_element_type | solution.py:43
  117.4 2.0 copy.102
  120.0 2.5 %broadcast_multiply_fusion = (f32[8,256,8,64]{1,0,3,2:T(8,128)S(1)}, f32[8,256,8,64]{1,0,3,2:T(8,128)}) fusion(f32[8,256,8]{1,0,2:T(8,128)S(1)} %copy.82, f32[8,256,8,64]{1,0,3,2:T(8,128)S(1)} %bitcast.112, f32[8,256,8]{1,0,2:T(8,128)S(1)} %copy.76), kind=kLoop, calls=%fused_computation.50 | loop fusion | flops 2097152 | bytes 12713984 | tf_op jit(solution)/shard_map/mul | solution.py:105
  122.5 3.0 %fusion.24 = f32[8,8,64,64]{3,2,1,0:T(8,128)S(1)} fusion(f32[8,256,8,64]{1,0,3,2:T(8,128)S(1)} %get-tuple-element.194, bf16[8,256,64,1]{1,0,2,3:T(8,128)(2,1)S(1)} %bitcast.120), kind=kOutput, calls=%fused_computation.40 | convolution fusion | flops 805306368 | bytes 5505024 | tf_op jit(solution)/shard_map/kshp,ksn->khpn/dot_general | solution.py:104
  125.5 6.8 %while.27 = (s32[]{:T(128)}, f32[8,64,64]{2,1,0:T(8,128)S(1)}, f32[8,8,64,64]{3,2,1,0:T(8,128)}, f32[8,8]{1,0:T(8,128)S(1)}, f32[8,8,64,64]{3,2,1,0:T(8,128)S(1)}, /*index=5*/s32[]{:T(128)}, s32[]{:T(128)}) while((s32[]{:T(128)}, f32[8,64,64]{2,1,0:T(8,128)S(1)}, f32[8,8,64,64]{3,2,1,0:T(8,128)}, f32[8,8]{1,0:T(8,128)S(1)}, ...), condition=%wide.region_3.4_spmd.clone, body=%wide.region_2.3_spmd.clone.sunk | while | flops 131075 | bytes 786636 | solution.py:113
  125.5 0.7 bitcast_dynamic-update-slice_fusion.2
  126.4 0.7 bitcast_dynamic-update-slice_fusion.2
  127.2 0.7 bitcast_dynamic-update-slice_fusion.2
  128.1 0.7 bitcast_dynamic-update-slice_fusion.2
  128.9 0.7 bitcast_dynamic-update-slice_fusion.2
  129.8 0.7 bitcast_dynamic-update-slice_fusion.2
  130.6 0.7 bitcast_dynamic-update-slice_fusion.2
  131.5 0.7 bitcast_dynamic-update-slice_fusion.2
  132.3 0.7 copy-done.4
  134.6 22.9 %all-reduce = f32[64]{0:T(128)S(1)} all-reduce(f32[64]{0:T(128)S(1)} %dynamic-update-slice), channel_id=2, replica_groups=mesh['seq'=8,'head'=4] {'seq'}, use_global_device_ids=true, to_apply=%add | all-reduce | flops 64 | bytes 512
  157.6 4.5 %copy.97 = bf16[2048,8,64]{0,2,1:T(8,128)(2,1)S(1)} copy(bf16[2048,8,64]{2,1,0:T(8,128)(2,1)} %get-tuple-element.199) | data formatting | bytes 4194304
  162.7 22.5 %fusion.2 = f32[8,8,64,256]{3,2,1,0:T(8,128)} fusion(f32[8,8,256]{2,1,0:T(8,128)S(1)} %add_bitcast_fusion.1, f32[8,256,256]{2,1,0:T(8,128)S(1)} %fusion.33, pred[256,256]{1,0:T(8,128)(4,1)S(1)} %iota_compare_fusion, f32[8,256,8,64]{1,0,3,2:T(8,128)} %get-tuple-element.195), kind=kOutput, calls=%fused_computation.7 | convolution fusion | flops 3238002688 | bytes 10616832 | tf_op jit(solution)/shard_map/khts,kshp->kthp/dot_general | solution.py:101
  185.2 8.8 %while.28 = (s32[]{:T(128)}, f32[8,64,64]{2,1,0:T(8,128)S(1)}, s32[]{:T(128)}, f32[8,8]{1,0:T(8,128)S(1)}, f32[8,8,64,64]{3,2,1,0:T(8,128)}, /*index=5*/s32[]{:T(128)}, s32[]{:T(128)}) while((s32[]{:T(128)}, f32[8,64,64]{2,1,0:T(8,128)S(1)}, s32[]{:T(128)}, f32[8,8]{1,0:T(8,128)S(1)}, f32[8,8,64,64]{3,2,1,0:T(8,128)}, ...), condition=%wide.region_7.8_spmd.clone, body=%wide.region_6.7_spmd.clone.sunk | while | flops 131076 | bytes 393425 | solution.py:36
  185.2 1.1 fusion.55
  186.3 1.1 fusion.55
  187.4 1.1 fusion.55
  188.5 1.1 fusion.55
  189.6 1.1 fusion.55
  190.7 1.1 fusion.55
  191.8 1.1 fusion.55
  192.9 1.1 fusion.55
  194.0 4.9 %fusion.23 = f32[8,8,8,8,256]{4,3,2,1,0:T(8,128)S(1)} fusion(f32[8,8,64,256]{3,2,1,0:T(8,128)} %fusion.2, f32[8,8,64,64]{3,2,1,0:T(8,128)} %get-tuple-element.127, f32[8,256,8]{1,2,0:T(8,128)S(1)} %get-tuple-element.192, f32[8,64,64]{2,1,0:T(8,128)S(1)} %get-tuple-element.129, f32[8,8]{1,0:T(8,128)S(1)} %get-tuple-element.202, ...), kind=kOutput, calls=%fused_computation.39 | convolution fusion | flops 807927808 | bytes 9896192 | tf_op jit(solution)/shard_map/ktn,khpn->kthp/dot_general | solution.py:126
  199.5 1.5 copy-done.3
  201.0 2.9 %fusion.27 = bf16[2048,8,64]{0,2,1:T(8,128)(2,1)} fusion(bf16[2048,8,64]{0,2,1:T(8,128)(2,1)S(1)} %copy.97, f32[2048,8,64]{0,2,1:T(8,128)S(1)} %bitcast.114, f32[2048,8,64]{0,2,1:T(8,128)S(1)} %bitcast.108, f32[8]{0:T(128)S(1)} %copy-done.10), kind=kLoop, calls=%fused_computation.44 | loop fusion | flops 9437184 | bytes 12582944 | tf_op jit(solution)/shard_map/convert_element_type | solution.py:134
  203.9 3.3 %all_to_all.35 = bf16[4,512,512]{1,0,2:T(4,128)(2,1)S(1)} reshape(bf16[2048,8,64]{0,2,1:T(8,128)(2,1)} %fusion.27) | data formatting | bytes 4194304 | tf_op jit(solution)/shard_map/all_to_all | solution.py:137
  207.7 28.2 %all_to_all.40 = bf16[4,512,512]{1,2,0:T(8,128)(2,1)S(1)} all-to-all(bf16[4,512,512]{1,2,0:T(8,128)(2,1)S(1)} %copy.88), channel_id=1, replica_groups=mesh['seq'=8,'head'=4] {'head'}, dimensions={0} | all-to-all | bytes 4194304 | tf_op jit(solution)/shard_map/all_to_all | solution.py:137
  236.9 1.1 copy-done.12
  238.0 3.4 %convolution_convert_fusion.1 = bf16[512,1024]{1,0:T(8,128)(2,1)} fusion(bf16[512,2048]{0,1:T(8,128)(2,1)S(1)} %fusion.22, bf16[2048,1024]{1,0:T(8,128)(2,1)S(1)} %copy-done.12), kind=kOutput, calls=%fused_computation.52 | convolution fusion | flops 2148007936 | bytes 7340032 | tf_op jit(solution)/shard_map/dot_general | solution.py:141
  (100 shorter events, 8.0 us)
Async XLA Ops:
  6.5 1.2 copy-start
  11.3 15.5 %all-to-all-start.1 = ((bf16[4,2,2048]{2,1,0:T(2,128)(2,1)}), bf16[4,2,2048]{2,1,0:T(2,128)(2,1)S(1)}, u32[]{:S(2)}, u32[]{:S(2)}) async-start(bf16[4,2,2048]{2,1,0:T(2,128)(2,1)} %reshape.184), calls=%async_computation.1 | async-start | bytes 65536 | tf_op jit(solution)/shard_map/all_to_all | solution.py:70
  26.8 5.1 %copy-start.6 = (f32[4,512]{1,0:T(4,128)S(1)}, f32[4,512]{1,0:T(4,128)}, u32[]{:S(2)}) copy-start(f32[4,512]{1,0:T(4,128)} %param.19) | copy-start | bytes 24580
  26.8 5.2 %copy-start.7 = (f32[4,128]{1,0:T(4,128)S(1)}, f32[4,128]{1,0:T(4,128)}, u32[]{:S(2)}) copy-start(f32[4,128]{1,0:T(4,128)} %param.21) | copy-start | bytes 6148
  26.8 5.2 %copy-start.8 = (f32[512]{0:T(512)S(1)}, f32[512]{0:T(512)}, u32[]{:S(2)}) copy-start(f32[512]{0:T(512)} %param.20) | copy-start | bytes 6148
  26.8 5.2 %copy-start.11 = (f32[128]{0:T(128)S(1)}, f32[128]{0:T(128)}, u32[]{:S(2)}) copy-start(f32[128]{0:T(128)} %param.22) | copy-start | bytes 1540
  26.8 56.8 %copy-start.13 = (f32[8]{0:T(128)S(1)}, f32[8]{0:T(128)}, u32[]{:S(2)}) copy-start(f32[8]{0:T(128)} %param.24) | copy-start | bytes 100
  26.8 56.9 %copy-start.9 = (f32[8]{0:T(128)S(1)}, f32[8]{0:T(128)}, u32[]{:S(2)}) copy-start(f32[8]{0:T(128)} %param.23) | copy-start | bytes 100
  26.8 62.3 %all-to-all-start = ((bf16[512,32,128]{2,0,1:T(8,128)(2,1)}), bf16[512,32,128]{2,0,1:T(8,128)(2,1)}, u32[]{:S(2)}, u32[]{:S(2)}) async-start(bf16[512,32,128]{2,0,1:T(8,128)(2,1)} %bitcast.113), calls=%async_computation | async-start | bytes 8388608 | tf_op jit(solution)/shard_map/all_to_all | solution.py:69
  31.8 153.4 %all-gather.4.cloned.1.call-start = ((), (), s32[]{:S(2)}) async-start(), calls=%async_computation.3 | async-start | bytes 2359296 | tf_op jit(solution)/shard_map/all_gather | solution.py:24
  102.6 7.9 %collective-permute-start = (bf16[3,640]{0,1:T(8,128)(2,1)S(1)}, bf16[3,640]{0,1:T(8,128)(2,1)S(1)}, u32[]{:S(2)}, u32[]{:S(2)}) collective-permute-start(bf16[3,640]{0,1:T(8,128)(2,1)S(1)} %pad_maximum_fusion), channel_id=1, source_target_pairs={{0,4},{4,8},{8,12},{12,16},{16,20},{20,24},{24,28},{1,5},{5,9},{9,... | collective-permute-start | bytes 11528 | tf_op jit(solution)/shard_map/ppermute | solution.py:19
  117.4 2.5 copy-start.2
  125.5 7.6 %copy-start.14 = (u32[32]{0:T(128)S(1)}, u32[32]{0:T(128)}, u32[]{:S(2)}) copy-start(u32[32]{0:T(128)} %constant.66) | copy-start | bytes 388
  132.3 0.7 copy-start.4
  198.8 2.2 copy-start.3
  198.9 2.2 copy-start.10
  207.7 28.7 %copy-start.5 = (f32[2048]{0:T(1024)S(1)}, f32[2048]{0:T(1024)}, u32[]{:S(2)}) copy-start(f32[2048]{0:T(1024)} %param.26) | copy-start | bytes 24580
  235.8 2.2 copy-start.12
  236.4 5.0 %copy-start.1 = (bf16[512,1024]{1,0:T(8,128)(2,1)S(1)}, bf16[512,1024]{1,0:T(8,128)(2,1)}, u32[]{:S(2)}) copy-start(bf16[512,1024]{1,0:T(8,128)(2,1)} %param.16) | copy-start | bytes 3145732
Sparse Core Ops, SparseCore 0:
  133.2 50.6 all-gather.3
where the time goes:
time: 249 us; the launch traced here: 248 us
  blocking collectives  103 us (41%)
  matrix products  43.9 us (18%)
  local copies, waits for them, and re-layouts  35.2 us (14%)
  other arithmetic  34.6 us (14%)
  between operations  14.5 us (6%)
  starting transfers between devices  13.4 us (5%)
  waiting for transfers between devices  3.71 us (1%)
    all_gather x1, blocking collectives, on_device(): bc_rows = lax.all_gather(bc_dt[:, :2 * STATE], 'head', axis=0, tiled=True)  51.6 us
    all_to_all x1, blocking collectives, on_device(): lax.all_to_all(gated_out, 'head', split_axis=0, concat_axis=1, tiled=True)  28.2 us
    unnamed x1, blocking collectives  22.9 us
    dot_general x1, matrix products, on_device(): jnp.einsum('khts,kshp->kthp', mixed, xdt_blocks, precision=highest)  22.5 us
    unnamed x42, local copies, waits for them, and re-layouts  13.7 us
    slice x2, local copies, waits for them, and re-layouts, on_device(): x_chan = gate_x[:, :, HEAD_DIM:].reshape(seq_rows, dinner_here)  8.42 us
    select_n x8, other arithmetic, hop(): return jax.tree.map(lambda a, b: jnp.where(reached, a, b), new, before)  8.42 us
    dot_general x1, matrix products, on_device(): jnp.dot(tokens, w_gate_x, preferred_element_type=jnp.float32)  8.12 us
  transfers between devices with their start and end apart: 4, of which 1 were waited for; matrix products, arithmetic and copies ran while one was open for 18% of the time, Pallas kernels for 0%

commit v1 on v0

v1 whole, which is shorter than its diff:
```python
import functools
import math

import jax
import jax.numpy as jnp
from jax import lax
from jax.experimental import pallas as pl
from jax.experimental.pallas import tpu as pltpu
from jax.sharding import PartitionSpec as P

HEADS = 32
HEAD_DIM = 64
STATE = 64
CONV = 4
QUADS = HEADS // 4
LANES = 4 * HEAD_DIM
HALF = 128
CHUNK = 128
HALO = 16
MSG = STATE + 16
EPSILON = 1e-05
LOG2E = math.log2(math.e)

f32, bf16 = jnp.float32, jnp.bfloat16
MESH = pl.DeviceIdType.MESH


def silu(x):
    half = 0.5 * x
    return half * (1.0 + jnp.tanh(half))


def dot(a, b, **kw):
    return jnp.dot(a, b, preferred_element_type=f32, **kw)


def iota(shape, dim):
    return lax.broadcasted_iota(jnp.int32, shape, dim)


def put(ref, at, state, factor):
    hi = factor.astype(bf16).astype(f32)
    first = iota((16, LANES), 0) < 8
    ref[(*at, pl.ds(0, STATE), slice(None))] = state.astype(bf16)
    ref[(*at, pl.ds(STATE, 16), slice(None))] = jnp.where(first, hi, factor - hi).astype(bf16)


def get(block):
    block = block.astype(f32)
    return block[:STATE], block[STATE : STATE + 1] + block[STATE + 8 : STATE + 9]


def group_of(n_seq):
    return 2 if n_seq % 2 == 0 else 1


def kernel(
    n_seq, n_head,
    tok_hbm, wg_hbm, wo_hbm, wbc_ref, cw_ref, cb_ref, cbcw_ref, cbcb_ref, dtb_ref, alog_ref, skip_ref, gain_ref,
    out_ref,
    tok, wbuf, wout, prm, bc_pad, bcv, cmat, bmat_t, six, cum_t, scores,
    xs, xbuf, xdt, cume, starts, msg, ybuf, gbuf,
    from_group, to_next, from_prev, to_group, sin,
    w_sem, l_sem, halo_sem, prm_sem, a_sem, b_sem, c_sem,
):
    T = tok_hbm.shape[0]
    n_chunk = T // CHUNK
    g_seq = group_of(n_seq)
    size, n_group = g_seq * n_head, n_seq // g_seq
    per = QUADS // size
    quads_in = QUADS // n_head
    here = HEADS // n_head
    seq, head = lax.axis_index("seq"), lax.axis_index("head")
    place, group = lax.rem(seq, g_seq) * n_head + head, seq // g_seq
    hops = [1 << k for k in range(n_group.bit_length()) if (1 << k) < n_group]

    def member(i):
        return (group * g_seq + i // n_head, lax.rem(i, n_head))

    wrap = head == n_head - 1
    next_device = (jnp.where(wrap, seq + 1, seq), jnp.where(wrap, 0, head + 1))
    has_next = jnp.logical_or(seq < n_seq - 1, head < n_head - 1)
    has_prev = jnp.logical_or(seq > 0, head > 0)

    tok_copy = pltpu.make_async_copy(tok_hbm, tok.at[pl.ds(HALO, T)], l_sem.at[0])
    tok_copy.start()

    def w_copy(q):
        cols = pl.ds(pl.multiple_of(q * 2 * LANES, 2 * LANES), 2 * LANES)
        return pltpu.make_async_copy(wg_hbm.at[:, cols], wbuf.at[q], w_sem.at[q])

    @pl.loop(0, QUADS)
    def _(q):
        w_copy(q).start()

    wo_copy = pltpu.make_async_copy(wo_hbm, wout, l_sem.at[1])
    wo_copy.start()

    barrier = pltpu.get_barrier_semaphore()

    def greet(cond, target):
        @pl.when(cond)
        def _():
            pl.semaphore_signal(barrier, inc=1, device_id=target, device_id_type=MESH)

    for o in range(1, size):
        pl.semaphore_signal(
            barrier, inc=1, device_id=member(lax.rem(place + o, size)), device_id_type=MESH
        )
    total = jnp.int32(size - 1)
    for d in hops:
        ahead, behind = group + d < n_group, group >= d
        greet(ahead, (seq + d * g_seq, head))
        greet(behind, (seq - d * g_seq, head))
        total = total + ahead.astype(jnp.int32) + behind.astype(jnp.int32)
    over = jnp.logical_and(place == size - 1, group < n_group - 1)
    under = jnp.logical_and(place == 0, group > 0)
    greet(over, (seq + 1, 0))
    greet(under, (seq - 1, n_head - 1))
    total = total + over.astype(jnp.int32) + under.astype(jnp.int32)

    wide = iota((1, LANES), 1)
    for k in range(quads_in):
        cols = slice(k * LANES, (k + 1) * LANES)
        at = head * quads_in + k
        prm[at, 0:CONV, :] = cw_ref[:, cols]
        prm[at, CONV : CONV + 1, :] = cb_ref[...].reshape(1, here * HEAD_DIM)[:, cols]
        skip = jnp.zeros((1, LANES), f32)
        vec_b, vec_a = skip, skip
        for i in range(4):
            skip = jnp.where(wide // HEAD_DIM == i, skip_ref[4 * k + i], skip)
        if k == 0:
            for i in range(here):
                mine = lax.rem(wide, HEADS) == head * here + i
                vec_b = jnp.where(mine, dtb_ref[i], vec_b)
                vec_a = jnp.where(mine, alog_ref[i], vec_a)
        prm[at, CONV + 1 : CONV + 2, :] = skip
        prm[at, CONV + 2 : CONV + 3, :] = vec_b
        prm[at, CONV + 3 : CONV + 4, :] = vec_a

    pl.semaphore_wait(barrier, total)

    def halo_copy():
        return pltpu.make_async_remote_copy(
            src_ref=tok_hbm.at[pl.ds(T - HALO, HALO)], dst_ref=tok.at[pl.ds(0, HALO)],
            send_sem=halo_sem.at[0], recv_sem=halo_sem.at[1],
            device_id=next_device, device_id_type=MESH,
        )

    @pl.when(has_next)
    def _():
        halo_copy().start()

    def prm_copy(o):
        block = prm.at[pl.ds(head * quads_in, quads_in)]
        return pltpu.make_async_remote_copy(
            src_ref=block, dst_ref=block,
            send_sem=prm_sem.at[0, o], recv_sem=prm_sem.at[1, o],
            device_id=(seq, lax.rem(head + o, n_head)), device_id_type=MESH,
        )

    for o in range(1, n_head):
        prm_copy(o).start()

    @pl.when(jnp.logical_not(has_prev))
    def _():
        tok[pl.ds(0, HALO), :] = jnp.zeros((HALO, tok.shape[1]), bf16)

    tok_copy.wait()

    @pl.when(has_prev)
    def _():
        halo_copy().wait_recv()

    @pl.when(has_next)
    def _():
        halo_copy().wait_send()

    for o in range(1, n_head):
        prm_copy(o).wait()

    w_dt = wbc_ref[2 * STATE :, :]
    w_bc = jnp.concatenate([wbc_ref[...], w_dt, w_dt, w_dt], axis=0)
    bc_dt = lax.dot_general(
        tok[...], w_bc, (((1,), (1,)), ((), ())), preferred_element_type=f32
    ).astype(bf16).astype(f32)
    bc_pad[...] = bc_dt[:, :HALF]
    acc = cbcb_ref[...].reshape(1, HALF)
    for k in range(CONV):
        acc = acc + cbcw_ref[pl.ds(k, 1), :] * bc_pad[pl.ds(HALO - CONV + 1 + k, T), :]
    bcv[...] = silu(acc).astype(bf16).astype(f32)
    head_prm = prm[0]
    for j in range(1, n_head):
        head_prm = head_prm + prm[j * quads_in]
    raw = bc_dt[HALO:, HALF:] + head_prm[CONV + 2 : CONV + 3, :HALF]
    dt = jnp.maximum(raw, 0.0) + jnp.log1p(jnp.exp(-jnp.abs(raw)))
    decay = dt * (-LOG2E * jnp.exp(head_prm[CONV + 3 : CONV + 4, :HALF]))

    def three(v):
        hi = v.astype(bf16).astype(f32)
        mid = (v - hi).astype(bf16).astype(f32)
        rest = v - hi - mid
        ln = iota(v.shape, 1)
        part = jnp.where(ln < 32, hi, jnp.where(ln < 64, mid, jnp.where(ln < 96, rest, 0.0)))
        return part.astype(bf16)

    six[:, 0:HALF] = three(dt)
    row, col = iota((CHUNK, CHUNK), 0), iota((CHUNK, CHUNK), 1)
    lower = row >= col
    tril = jnp.where(lower, 1.0, 0.0)
    for c in range(n_chunk):
        rows = slice(c * CHUNK, (c + 1) * CHUNK)
        cum = dot(tril, decay[rows], precision=lax.Precision.HIGHEST)
        six[rows, HALF:] = three(cum)
        cum_t[c] = cum.T
        both = bcv[rows, :]
        flipped = both.T
        bmat_t[:, rows] = flipped[:STATE].astype(bf16)
        c_c = both[:, STATE:].astype(bf16)
        cmat[rows, :] = c_c
        scores[c] = jnp.where(lower, dot(c_c, flipped[:STATE].astype(bf16)), 0.0)

    def half_of(q, first):
        cuts = [slice(2 * HEAD_DIM * i + first, 2 * HEAD_DIM * i + first + HEAD_DIM) for i in range(4)]
        return jnp.concatenate([wbuf[q, :, cut] for cut in cuts], axis=1)

    def a_copy(owner, slot):
        return pltpu.make_async_remote_copy(
            src_ref=msg.at[pl.ds(owner * per, per)], dst_ref=from_group.at[slot],
            send_sem=a_sem.at[0, owner], recv_sem=a_sem.at[1, slot],
            device_id=member(owner), device_id_type=MESH,
        )

    @pl.loop(0, QUADS)
    def _(q):
        w_copy(q).wait()
        pq = prm[q]
        xs[...] = dot(tok[...], half_of(q, HEAD_DIM)).astype(bf16).astype(f32)
        r6, l6 = iota((HALF, LANES), 0), iota((HALF, LANES), 1)
        spread = jnp.where((r6 & 31) == 4 * q + (l6 >> 6), 1.0, 0.0).astype(bf16)
        state = jnp.zeros((STATE, LANES), f32)
        whole = jnp.zeros((1, LANES), f32)
        for c in range(n_chunk):
            rows = slice(c * CHUNK, (c + 1) * CHUNK)
            acc = pq[CONV : CONV + 1]
            for k in range(CONV):
                acc = acc + pq[k : k + 1] * xs[pl.ds(HALO - CONV + 1 + k + c * CHUNK, CHUNK), :]
            xc = silu(acc).astype(bf16)
            xbuf[q, rows, :] = xc
            xd = xc.astype(f32) * dot(six[rows, :HALF], spread)
            ce = dot(six[rows, HALF:], spread)
            xdt[q, rows, :] = xd.astype(bf16)
            cume[q, rows, :] = ce
            end = ce[CHUNK - 1 : CHUNK]
            starts[q, c] = state.astype(bf16)
            weighted = (jnp.exp2(end - ce) * xd).astype(bf16)
            state = jnp.exp2(end) * state + dot(bmat_t[:, rows], weighted)
            whole = whole + end
        put(msg, (q,), state, jnp.exp2(whole))
        owner = q // per

        @pl.when(jnp.logical_and(lax.rem(q, per) == per - 1, owner != place))
        def _():
            a_copy(owner, place).start()

    from_group[place] = msg[pl.ds(place * per, per)]

    def intra(first, last):
        @pl.loop(first, last)
        def _(q):
            skip = prm[q, CONV + 1 : CONV + 2]
            w_z = half_of(q, 0)
            off = jnp.zeros((1, LANES), f32)
            for c in range(n_chunk):
                rows = pl.ds(c * CHUNK, CHUNK)
                z = dot(tok[pl.ds(HALO + c * CHUNK, CHUNK), :], w_z).astype(bf16).astype(f32)
                gate = silu(z)
                ce = cume[q, rows, :]
                s_c = scores[c]
                x_c = xdt[q, rows, :]
                y_parts = []
                for pair in range(2):
                    parts = []
                    for odd in range(2):
                        i = 2 * pair + odd
                        gap = ce[:, i * HEAD_DIM : i * HEAD_DIM + 1] - cum_t[c, pl.ds(4 * q + i, 1), :]
                        parts.append((s_c * jnp.exp2(jnp.minimum(gap, 0.0))).astype(bf16))
                    x_p = x_c[:, pair * HALF : (pair + 1) * HALF].astype(f32)
                    lo_c = iota(x_p.shape, 1) < HEAD_DIM
                    right = jnp.concatenate(
                        [jnp.where(lo_c, x_p, 0.0).astype(bf16), jnp.where(lo_c, 0.0, x_p).astype(bf16)], axis=0
                    )
                    y_parts.append(dot(jnp.concatenate(parts, axis=1), right))
                y = jnp.concatenate(y_parts, axis=1)
                y = y + jnp.exp2(ce) * dot(cmat[rows, :], starts[q, c])
                ybuf[q, rows, :] = (y + skip * xbuf[q, rows, :].astype(f32)) * gate
                cume[q, rows, :] = jnp.exp2(ce + off) * gate
                off = off + ce[CHUNK - 1 : CHUNK]

    slots = len(hops) + 2
    cuts = [QUADS * k // slots for k in range(slots + 1)]
    intra(cuts[0], cuts[1])

    for o in range(size):
        @pl.when(place != o)
        def _():
            a_copy(jnp.int32(o), o).wait()

    none = (jnp.zeros((STATE, LANES), f32), jnp.ones((1, LANES), f32))
    inc, before = [], []
    for p in range(per):
        state, factor = none
        mine = []
        for j in range(size):
            mine.append((state, factor))
            s_j, f_j = get(from_group[j, p])
            state, factor = f_j * state + s_j, factor * f_j
        before.append(mine)
        inc.append((state, factor))
    exc = [none for _ in range(per)]

    def b_copy(k):
        return pltpu.make_async_remote_copy(
            src_ref=to_next.at[k], dst_ref=from_prev.at[k],
            send_sem=b_sem.at[0, k], recv_sem=b_sem.at[1, k],
            device_id=(seq + hops[k] * g_seq, head), device_id_type=MESH,
        )

    for k, d in enumerate(hops):
        for p in range(per):
            put(to_next, (k, p), *inc[p])

        @pl.when(group + d < n_group)
        def _():
            b_copy(k).start()

        @pl.when(group < d)
        def _():
            for p in range(per):
                put(from_prev, (k, p), *none)

        intra(cuts[k + 1], cuts[k + 2])

        @pl.when(group >= d)
        def _():
            b_copy(k).wait_recv()

        @pl.when(group + d < n_group)
        def _():
            b_copy(k).wait_send()

        for p in range(per):
            s_r, f_r = get(from_prev[k, p])
            (s_i, f_i), (s_e, f_e) = inc[p], exc[p]
            inc[p] = (s_i + f_i * s_r, f_i * f_r)
            exc[p] = (s_e + f_e * s_r, f_e * f_r)

    for j in range(size):
        for p in range(per):
            s_b, f_b = before[p][j]
            to_group[j, p] = (s_b + f_b * exc[p][0]).astype(bf16)

    def c_copy(o, slot):
        return pltpu.make_async_remote_copy(
            src_ref=to_group.at[o], dst_ref=sin.at[slot],
            send_sem=c_sem.at[0, o], recv_sem=c_sem.at[1, slot],
            device_id=member(o), device_id_type=MESH,
        )

    for o in range(size):
        @pl.when(place != o)
        def _():
            c_copy(jnp.int32(o), place).start()

    sin[place] = to_group[place]
    intra(cuts[-2], cuts[-1])
    for o in range(size):
        @pl.when(place != o)
        def _():
            c_copy(jnp.int32(o), o).wait()

    def finish(q, squares):
        gated = ybuf[q] + cume[q] * dot(cmat[...], sin[q // per, lax.rem(q, per)])
        gated = gated.astype(bf16).astype(f32)
        cols = pl.ds(pl.multiple_of(q * LANES, LANES), LANES)
        gbuf[:, cols] = (gated * gain_ref[cols].reshape(1, LANES)).astype(bf16)
        squared = gated * gated
        return squares + squared[:, :HALF] + squared[:, HALF:]

    squares = lax.fori_loop(0, QUADS, finish, jnp.zeros((T, HALF), f32))
    mean_sq = jnp.sum(squares, axis=1, keepdims=True) * (1.0 / (HEADS * HEAD_DIM))
    scale = lax.rsqrt(mean_sq + EPSILON)
    wo_copy.wait()
    width = out_ref.shape[1]
    for n in range(width // 256):
        cols = slice(n * 256, (n + 1) * 256)
        out_ref[:, cols] = (dot(gbuf[...], wout[:, cols]) * scale).astype(bf16)


def on_device(
    n_seq, n_head,
    tokens, w_gate_x, w_bc_dt, conv_x_weight, conv_x_bias, conv_bc_weight, conv_bc_bias,
    dt_bias, a_log, skip_d, norm_gain, w_out,
):
    T, width = tokens.shape
    g_seq = group_of(n_seq)
    size = g_seq * n_head
    per = QUADS // size
    n_hops = max(1, (n_seq // g_seq - 1).bit_length())
    n_chunk = T // CHUNK
    vmem, any_ = pl.BlockSpec(memory_space=pltpu.VMEM), pl.BlockSpec(memory_space=pl.ANY)
    smem = pl.BlockSpec(memory_space=pltpu.SMEM)
    dma = pltpu.SemaphoreType.DMA
    return pl.pallas_call(
        functools.partial(kernel, n_seq, n_head),
        out_shape=jax.ShapeDtypeStruct((T, width), bf16),
        in_specs=[any_, any_, any_, vmem, vmem, vmem, vmem, vmem, smem, smem, smem, vmem],
        out_specs=vmem,
        scratch_shapes=[
            pltpu.VMEM((HALO + T, width), bf16),
            pltpu.VMEM((QUADS, width, 2 * LANES), bf16),
            pltpu.VMEM(w_out.shape, bf16),
            pltpu.VMEM((QUADS, 8, LANES), f32),
            pltpu.VMEM((HALO + T, HALF), f32),
            pltpu.VMEM((T, HALF), f32),
            pltpu.VMEM((T, STATE), bf16),
            pltpu.VMEM((STATE, T), bf16),
            pltpu.VMEM((T, 2 * HALF), bf16),
            pltpu.VMEM((n_chunk, HALF, CHUNK), f32),
            pltpu.VMEM((n_chunk, CHUNK, CHUNK), f32),
            pltpu.VMEM((HALO + T, LANES), f32),
            pltpu.VMEM((QUADS, T, LANES), bf16),
            pltpu.VMEM((QUADS, T, LANES), bf16),
            pltpu.VMEM((QUADS, T, LANES), f32),
            pltpu.VMEM((QUADS, n_chunk, STATE, LANES), bf16),
            pltpu.VMEM((QUADS, MSG, LANES), bf16),
            pltpu.VMEM((QUADS, T, LANES), f32),
            pltpu.VMEM((T, HEADS * HEAD_DIM), bf16),
            pltpu.VMEM((size, per, MSG, LANES), bf16),
            pltpu.VMEM((n_hops, per, MSG, LANES), bf16),
            pltpu.VMEM((n_hops, per, MSG, LANES), bf16),
            pltpu.VMEM((size, per, STATE, LANES), bf16),
            pltpu.VMEM((size, per, STATE, LANES), bf16),
            dma((QUADS,)),
            dma((2,)),
            dma((2,)),
            dma((2, n_head)),
            dma((2, size)),
            dma((2, n_hops)),
            dma((2, size)),
        ],
        compiler_params=pltpu.CompilerParams(
            collective_id=0, has_side_effects=True, vmem_limit_bytes=56 * 1024 * 1024
        ),
        cost_estimate=pl.CostEstimate(
            flops=2 * T * width * 6500, bytes_accessed=14 * 1024 * 1024, transcendentals=0
        ),
    )(
        tokens, w_gate_x, w_out, w_bc_dt.T, conv_x_weight, conv_x_bias, conv_bc_weight, conv_bc_bias,
        dt_bias, a_log, skip_d, norm_gain,
    )


def solution(mesh):
    return jax.shard_map(
        functools.partial(on_device, mesh.shape["seq"], mesh.shape["head"]),
        mesh=mesh,
        in_specs=(
            P(("seq", "head"), None),
            P(),
            P(),
            P(None, "head"),
            P("head"),
            P(),
            P(),
            P("head"),
            P("head"),
            P("head"),
            P(),
            P(),
        ),
        out_specs=P(("seq", "head"), None),
        check_vma=False,
    )
```

time: 249 us -> 42.8 us (0.17)
  blocking collectives: 103 us -> 0 us
  matrix products: 43.9 us -> 0 us
  Pallas kernels: 0 us -> 40.3 us
  other arithmetic: 34.6 us -> 0 us
  local copies, waits for them, and re-layouts: 35.2 us -> 2.26 us
  between operations: 14.5 us -> 0.01 us
  starting transfers between devices: 13.4 us -> 0 us
  waiting for transfers between devices: 3.71 us -> 0 us
    all_gather x1 -> x0, blocking collectives: 51.6 us -> none  [on_device(): bc_rows = lax.all_gather(bc_dt[:, :2 * STATE], 'head', axis=0, tiled=True)]
    dot_general x7 -> x0, matrix products: 43.9 us -> none  [the longest x1 22.5 us: on_device(): jnp.einsum('khts,kshp->kthp', mixed, xdt_blocks, precision=highest)]
    pallas_call x0 -> x1, Pallas kernels: none -> 40.3 us  [on_device(): pl.pallas_call(functools.partial(kernel, n_seq, n_head), out_shape=jax.Sh...]
    all_to_all x1 -> x0, blocking collectives: 28.2 us -> none  [on_device(): lax.all_to_all(gated_out, 'head', split_axis=0, concat_axis=1, tiled=True)]
    unnamed x1 -> x0, blocking collectives: 22.9 us -> none
    unnamed x42 -> x1, local copies, waits for them, and re-layouts: 13.7 us -> 2.26 us
    convert_element_type x5 -> x0, other arithmetic: 10.3 us -> none  [the longest x1 5.21 us: causal_taps(): return jax.nn.silu(summed).astype(jnp.bfloat16)]
    all_to_all x2 -> x0, starting transfers between devices: 9.21 us -> none  [the longest x1 5 us: on_device(): lax.all_to_all(gate_all, 'head', split_axis=1, concat_axis=0, tiled=True)]
  transfers between devices with their start and end apart: 4 -> 0, of which waited for: 1 -> 0; matrix products, arithmetic and copies ran while one was open for 18% -> 0% of each run, Pallas kernels for 0% -> 0%
where the time goes in v1:
time: 42.8 us; the launch traced here: 42.6 us
  Pallas kernels  40.3 us (94%)
  local copies, waits for them, and re-layouts  2.26 us (5%)
    pallas_call x1, Pallas kernels, on_device(): pl.pallas_call(functools.partial(kernel, n_seq, n_head), out_shape=jax.Sh...  40.3 us
    unnamed x1, local copies, waits for them, and re-layouts  2.26 us

profile of v1, /device:TPU:0, one launch (start us, length us, event | category | flops | bytes accessed | tf_op | source)
XLA Modules:
  0.0 42.6 jit_solution(1052964714983806785)
XLA Ops:
  0.0 40.3 %shard_map.118 = bf16[512,1024]{1,0:T(8,128)(2,1)} custom-call(bf16[512,1024]{1,0:T(8,128)(2,1)} %tok_hbm.1, bf16[1024,4096]{1,0:T(8,128)(2,1)} %wg_hbm.1, bf16[2048,1024]{1,0:T(8,128)(2,1)} %wo_hbm.1, bf16[160,1024]{1,0:T(8,128)(2,1)} %bitcast.1, f32[4,512]{1,0:T(4,128)} %cw_ref.1, f32[512]{0:T(512)} %cb_ref.1, f32[4,128]{1,0:T(4,128)} %cbcw_ref.1, ...), custom_call_target="tpu_custom_call" | custom-call | flops 6815744000 | bytes 14680064 | tf_op jit(solution)/shard_map/pallas_call | solution.py:414
  40.4 2.3 %copy.14 = bf16[512,1024]{1,0:T(8,128)(2,1)} copy(bf16[512,1024]{1,0:T(8,128)(2,1)} %shard_map.118) | data formatting | bytes 2097152

commit v2 on v1

--- a/solution.py
+++ b/solution.py
@@ -59,8 +59,8 @@
     tok_hbm, wg_hbm, wo_hbm, wbc_ref, cw_ref, cb_ref, cbcw_ref, cbcb_ref, dtb_ref, alog_ref, skip_ref, gain_ref,
     out_ref,
     tok, wbuf, wout, prm, bc_pad, bcv, cmat, bmat_t, six, cum_t, scores,
-    xs, xbuf, xdt, cume, starts, msg, ybuf, gbuf,
-    from_group, to_next, from_prev, to_group, sin,
+    buf_a, buf_b, zs_a, zs_b, xbuf, xdt, cume, starts, msg, ybuf, gbuf,
+    from_group, to_next, from_prev, to_group, sin, before, run,
     w_sem, l_sem, halo_sem, prm_sem, a_sem, b_sem, c_sem,
 ):
     T = tok_hbm.shape[0]
@@ -231,13 +231,20 @@
             device_id=member(owner), device_id_type=MESH,
         )
 
-    @pl.loop(0, QUADS)
-    def _(q):
+    def project_x(q, xs):
         w_copy(q).wait()
+        xs[...] = dot(tok[...], half_of(q, HEAD_DIM)).astype(bf16).astype(f32)
+
+    def project_z(q, zs):
+        zs[...] = dot(tok[pl.ds(HALO, T), :], half_of(q, 0)).astype(bf16).astype(f32)
+
+    def states(q, xs):
         pq = prm[q]
-        xs[...] = dot(tok[...], half_of(q, HEAD_DIM)).astype(bf16).astype(f32)
         r6, l6 = iota((HALF, LANES), 0), iota((HALF, LANES), 1)
         spread = jnp.where((r6 & 31) == 4 * q + (l6 >> 6), 1.0, 0.0).astype(bf16)
+        steps = dot(six[:, :HALF], spread)
+        cums = dot(six[:, HALF:], spread)
+        cume[q] = cums
         state = jnp.zeros((STATE, LANES), f32)
         whole = jnp.zeros((1, LANES), f32)
         for c in range(n_chunk):
@@ -247,77 +254,43 @@
                 acc = acc + pq[k : k + 1] * xs[pl.ds(HALO - CONV + 1 + k + c * CHUNK, CHUNK), :]
             xc = silu(acc).astype(bf16)
             xbuf[q, rows, :] = xc
-            xd = xc.astype(f32) * dot(six[rows, :HALF], spread)
-            ce = dot(six[rows, HALF:], spread)
+            xd = xc.astype(f32) * steps[rows]
+            ce = cums[rows]
             xdt[q, rows, :] = xd.astype(bf16)
-            cume[q, rows, :] = ce
             end = ce[CHUNK - 1 : CHUNK]
             starts[q, c] = state.astype(bf16)
             weighted = (jnp.exp2(end - ce) * xd).astype(bf16)
             state = jnp.exp2(end) * state + dot(bmat_t[:, rows], weighted)
             whole = whole + end
         put(msg, (q,), state, jnp.exp2(whole))
-        owner = q // per
-
-        @pl.when(jnp.logical_and(lax.rem(q, per) == per - 1, owner != place))
-        def _():
-            a_copy(owner, place).start()
-
-    from_group[place] = msg[pl.ds(place * per, per)]
-
-    def intra(first, last):
-        @pl.loop(first, last)
-        def _(q):
-            skip = prm[q, CONV + 1 : CONV + 2]
-            w_z = half_of(q, 0)
-            off = jnp.zeros((1, LANES), f32)
-            for c in range(n_chunk):
-                rows = pl.ds(c * CHUNK, CHUNK)
-                z = dot(tok[pl.ds(HALO + c * CHUNK, CHUNK), :], w_z).astype(bf16).astype(f32)
-                gate = silu(z)
-                ce = cume[q, rows, :]
-                s_c = scores[c]
-                x_c = xdt[q, rows, :]
-                y_parts = []
-                for pair in range(2):
-                    parts = []
-                    for odd in range(2):
-                        i = 2 * pair + odd
-                        gap = ce[:, i * HEAD_DIM : i * HEAD_DIM + 1] - cum_t[c, pl.ds(4 * q + i, 1), :]
-                        parts.append((s_c * jnp.exp2(jnp.minimum(gap, 0.0))).astype(bf16))
-                    x_p = x_c[:, pair * HALF : (pair + 1) * HALF].astype(f32)
-                    lo_c = iota(x_p.shape, 1) < HEAD_DIM
-                    right = jnp.concatenate(
-                        [jnp.where(lo_c, x_p, 0.0).astype(bf16), jnp.where(lo_c, 0.0, x_p).astype(bf16)], axis=0
-                    )
-                    y_parts.append(dot(jnp.concatenate(parts, axis=1), right))
-                y = jnp.concatenate(y_parts, axis=1)
-                y = y + jnp.exp2(ce) * dot(cmat[rows, :], starts[q, c])
-                ybuf[q, rows, :] = (y + skip * xbuf[q, rows, :].astype(f32)) * gate
-                cume[q, rows, :] = jnp.exp2(ce + off) * gate
-                off = off + ce[CHUNK - 1 : CHUNK]
-
-    slots = len(hops) + 2
-    cuts = [QUADS * k // slots for k in range(slots + 1)]
-    intra(cuts[0], cuts[1])
-
-    for o in range(size):
-        @pl.when(place != o)
-        def _():
-            a_copy(jnp.int32(o), o).wait()
-
-    none = (jnp.zeros((STATE, LANES), f32), jnp.ones((1, LANES), f32))
-    inc, before = [], []
-    for p in range(per):
-        state, factor = none
-        mine = []
-        for j in range(size):
-            mine.append((state, factor))
-            s_j, f_j = get(from_group[j, p])
-            state, factor = f_j * state + s_j, factor * f_j
-        before.append(mine)
-        inc.append((state, factor))
-    exc = [none for _ in range(per)]
+
+    def intra(q, zs):
+        skip = prm[q, CONV + 1 : CONV + 2]
+        off = jnp.zeros((1, LANES), f32)
+        for c in range(n_chunk):
+            rows = pl.ds(c * CHUNK, CHUNK)
+            gate = silu(zs[rows, :])
+            ce = cume[q, rows, :]
+            s_c = scores[c]
+            x_c = xdt[q, rows, :]
+            y_parts = []
+            for pair in range(2):
+                parts = []
+                for odd in range(2):
+                    i = 2 * pair + odd
+                    gap = ce[:, i * HEAD_DIM : i * HEAD_DIM + 1] - cum_t[c, pl.ds(4 * q + i, 1), :]
+                    parts.append((s_c * jnp.exp2(jnp.minimum(gap, 0.0))).astype(bf16))
+                x_p = x_c[:, pair * HALF : (pair + 1) * HALF].astype(f32)
+                lo_c = iota(x_p.shape, 1) < HEAD_DIM
+                right = jnp.concatenate(
+                    [jnp.where(lo_c, x_p, 0.0).astype(bf16), jnp.where(lo_c, 0.0, x_p).astype(bf16)], axis=0
+                )
+                y_parts.append(dot(jnp.concatenate(parts, axis=1), right))
+            y = jnp.concatenate(y_parts, axis=1)
+            y = y + jnp.exp2(ce) * dot(cmat[rows, :], starts[q, c])
+            ybuf[q, rows, :] = (y + skip * xbuf[q, rows, :].astype(f32)) * gate
+            cume[q, rows, :] = jnp.exp2(ce + off) * gate
+            off = off + ce[CHUNK - 1 : CHUNK]
 
     def b_copy(k):
         return pltpu.make_async_remote_copy(
@@ -326,40 +299,6 @@
             device_id=(seq + hops[k] * g_seq, head), device_id_type=MESH,
         )
 
-    for k, d in enumerate(hops):
-        for p in range(per):
-            put(to_next, (k, p), *inc[p])
-
-        @pl.when(group + d < n_group)
-        def _():
-            b_copy(k).start()
-
-        @pl.when(group < d)
-        def _():
-            for p in range(per):
-                put(from_prev, (k, p), *none)
-
-        intra(cuts[k + 1], cuts[k + 2])
-
-        @pl.when(group >= d)
-        def _():
-            b_copy(k).wait_recv()
-
-        @pl.when(group + d < n_group)
-        def _():
-            b_copy(k).wait_send()
-
-        for p in range(per):
-            s_r, f_r = get(from_prev[k, p])
-            (s_i, f_i), (s_e, f_e) = inc[p], exc[p]
-            inc[p] = (s_i + f_i * s_r, f_i * f_r)
-            exc[p] = (s_e + f_e * s_r, f_e * f_r)
-
-    for j in range(size):
-        for p in range(per):
-            s_b, f_b = before[p][j]
-            to_group[j, p] = (s_b + f_b * exc[p][0]).astype(bf16)
-
     def c_copy(o, slot):
         return pltpu.make_async_remote_copy(
             src_ref=to_group.at[o], dst_ref=sin.at[slot],
@@ -367,16 +306,123 @@
             device_id=member(o), device_id_type=MESH,
         )
 
+    none = (jnp.zeros((STATE, LANES), f32), jnp.ones((1, LANES), f32))
+
+    def scan_step(step):
+        if step == 0:
+            from_group[place] = msg[pl.ds(place * per, per)]
+            for o in range(size):
+                @pl.when(place != o)
+                def _():
+                    a_copy(jnp.int32(o), o).wait_recv()
+
+            for p in range(per):
+                state, factor = none
+                for j in range(size):
+                    before[j, p, 0:STATE, :] = state
+                    before[j, p, pl.ds(STATE, 8), :] = jnp.broadcast_to(factor, (8, LANES))
+                    s_j, f_j = get(from_group[j, p])
+                    state, factor = f_j * state + s_j, factor * f_j
+                total = (state, factor)
+                for at, (s, f) in ((0, total), (1, none)):
+                    run[at, p, 0:STATE, :] = s
+                    run[at, p, pl.ds(STATE, 8), :] = jnp.broadcast_to(f, (8, LANES))
+        else:
+            k = step - 1
+
+            @pl.when(group >= hops[k])
+            def _():
+                b_copy(k).wait_recv()
+
+            @pl.when(group + hops[k] < n_group)
+            def _():
+                b_copy(k).wait_send()
+
+            for p in range(per):
+                s_r, f_r = get(from_prev[k, p])
+                for at in range(2):
+                    f = run[at, p, pl.ds(STATE, 1), :]
+                    run[at, p, 0:STATE, :] = run[at, p, 0:STATE, :] + f * s_r
+                    run[at, p, pl.ds(STATE, 8), :] = jnp.broadcast_to(f * f_r, (8, LANES))
+        if step < len(hops):
+            d = hops[step]
+            for p in range(per):
+                put(to_next, (step, p), run[0, p, 0:STATE, :], run[0, p, pl.ds(STATE, 1), :])
+
+            @pl.when(group + d < n_group)
+            def _():
+                b_copy(step).start()
+
+            @pl.when(group < d)
+            def _():
+                for p in range(per):
+                    put(from_prev, (step, p), *none)
+        else:
+            for j in range(size):
+                for p in range(per):
+                    f_b = before[j, p, pl.ds(STATE, 1), :]
+                    value = before[j, p, 0:STATE, :] + f_b * run[1, p, 0:STATE, :]
+                    to_group[j, p] = value.astype(bf16)
+            for o in range(size):
+                @pl.when(place != o)
+                def _():
+                    c_copy(jnp.int32(o), place).start()
+
+            sin[place] = to_group[place]
+
+    ready = ((place + 1) * per - 1) // 2
+
+    def scan_steps(slot):
+        for step in range(len(hops) + 1):
+            @pl.when(slot == ready + 1 + step)
+            def _():
+                scan_step(step)
+
+    def send_states(i):
+        for k in range(2):
+            q = 2 * i + k
+            owner = q // per
+
+            @pl.when(jnp.logical_and(lax.rem(q, per) == per - 1, owner != place))
+            def _():
+                a_copy(owner, place).start()
+
+    n_body = QUADS // 2
+    project_x(0, buf_a)
+
+    @pl.loop(0, n_body - 1)
+    def _(i):
+        project_x(2 * i + 1, buf_b)
+        states(2 * i, buf_a)
+        project_x(2 * i + 2, buf_a)
+        states(2 * i + 1, buf_b)
+        send_states(i)
+        scan_steps(i)
+
+    project_x(QUADS - 1, buf_b)
+    states(QUADS - 2, buf_a)
+    project_z(0, zs_a)
+    states(QUADS - 1, buf_b)
+    send_states(n_body - 1)
+    scan_steps(n_body - 1)
+
+    @pl.loop(0, n_body - 1)
+    def _(i):
+        project_z(2 * i + 1, zs_b)
+        intra(2 * i, zs_a)
+        project_z(2 * i + 2, zs_a)
+        intra(2 * i + 1, zs_b)
+        scan_steps(n_body + i)
+
+    project_z(QUADS - 1, zs_b)
+    intra(QUADS - 2, zs_a)
+    intra(QUADS - 1, zs_b)
+    for late in range(2 * n_body - 1, n_body + len(hops) + 1):
+        scan_steps(late)
     for o in range(size):
         @pl.when(place != o)
         def _():
-            c_copy(jnp.int32(o), place).start()
-
-    sin[place] = to_group[place]
-    intra(cuts[-2], cuts[-1])
-    for o in range(size):
-        @pl.when(place != o)
-        def _():
+            a_copy(jnp.int32(o), o).wait_send()
             c_copy(jnp.int32(o), o).wait()
 
     def finish(q, squares):
@@ -429,6 +475,9 @@
             pltpu.VMEM((n_chunk, HALF, CHUNK), f32),
             pltpu.VMEM((n_chunk, CHUNK, CHUNK), f32),
             pltpu.VMEM((HALO + T, LANES), f32),
+            pltpu.VMEM((HALO + T, LANES), f32),
+            pltpu.VMEM((T, LANES), f32),
+            pltpu.VMEM((T, LANES), f32),
             pltpu.VMEM((QUADS, T, LANES), bf16),
             pltpu.VMEM((QUADS, T, LANES), bf16),
             pltpu.VMEM((QUADS, T, LANES), f32),
@@ -441,6 +490,8 @@
             pltpu.VMEM((n_hops, per, MSG, LANES), bf16),
             pltpu.VMEM((size, per, STATE, LANES), bf16),
             pltpu.VMEM((size, per, STATE, LANES), bf16),
+            pltpu.VMEM((size, per, STATE + 8, LANES), f32),
+            pltpu.VMEM((2, per, STATE + 8, LANES), f32),
             dma((QUADS,)),
             dma((2,)),
             dma((2,)),

time: 42.8 us -> 45.6 us (1.065); the launches traced: 42.6 us -> 44.8 us
  Pallas kernels: 40.3 us -> 42.5 us
    pallas_call x1, Pallas kernels: 40.3 us -> 42.5 us  [on_device(): pl.pallas_call(functools.partial(kernel, n_seq, n_head), out_shape=jax.Sh...]
where the time goes in v2:
time: 45.6 us; the launch traced here: 44.8 us
  Pallas kernels  42.5 us (93%)
  local copies, waits for them, and re-layouts  2.26 us (5%)
    pallas_call x1, Pallas kernels, on_device(): pl.pallas_call(functools.partial(kernel, n_seq, n_head), out_shape=jax.Sh...  42.5 us
    unnamed x1, local copies, waits for them, and re-layouts  2.26 us

profile of v2, /device:TPU:0, one launch (start us, length us, event | category | flops | bytes accessed | tf_op | source)
XLA Modules:
  0.0 44.8 jit_solution(7607460896323017905)
XLA Ops:
  0.0 42.5 %shard_map.118 = bf16[512,1024]{1,0:T(8,128)(2,1)} custom-call(bf16[512,1024]{1,0:T(8,128)(2,1)} %tok_hbm.1, bf16[1024,4096]{1,0:T(8,128)(2,1)} %wg_hbm.1, bf16[2048,1024]{1,0:T(8,128)(2,1)} %wo_hbm.1, bf16[160,1024]{1,0:T(8,128)(2,1)} %bitcast.1, f32[4,512]{1,0:T(4,128)} %cw_ref.1, f32[512]{0:T(512)} %cb_ref.1, f32[4,128]{1,0:T(4,128)} %cbcw_ref.1, ...), custom_call_target="tpu_custom_call" | custom-call | flops 6815744000 | bytes 14680064 | tf_op jit(solution)/shard_map/pallas_call | solution.py:460
  42.5 2.3 %copy.14 = bf16[512,1024]{1,0:T(8,128)(2,1)} copy(bf16[512,1024]{1,0:T(8,128)(2,1)} %shard_map.118) | data formatting | bytes 2097152
